TPU v7x, 32 devices: a whole 2x2x4 slice. The times are simulated.
32 devices in a mesh: groups: 2 (over y), dp: 4 (over z), expert: 4 (over x, core).
Axes of the slice: x: 2, y: 2, z: 4, core: 2. Of those that a mesh axis runs over, the one named last changes fastest.
Arguments:
- tokens: bfloat16 [4096, 4096], P(('groups', 'dp', 'expert')), parts along dimension 0, may hold values from -20 to 20
- cotangent: bfloat16 [4096, 4096], P(('groups', 'dp', 'expert')), parts along dimension 0, may hold values from -24 to 24
- router_weight: bfloat16 [8192, 64], P('groups'), parts along dimension 0, may hold values from -0.0625 to 0.0625
- w_gate: bfloat16 [8192, 16384], P('groups', ('dp', 'expert')), parts along dimension 0, may hold values from -0.09375 to 0.09375
- w_up: bfloat16 [8192, 16384], P('groups', ('dp', 'expert')), parts along dimension 0, may hold values from -0.09375 to 0.09375
- w_down: bfloat16 [32768, 4096], P(('groups', 'dp', 'expert')), parts along dimension 0, may hold values from -0.046875 to 0.046875
- slot_token: int32 [128], P('groups'), parts along dimension 0, may hold values from 0 to 2047, as said below
Outputs:
- d_tokens: bfloat16 [4096, 4096], P(('groups', 'dp', 'expert')), parts along dimension 0
- d_router: float32 [8192, 64], P('groups'), parts along dimension 0
- d_w_gate: bfloat16 [8192, 16384], P('groups', ('dp', 'expert')), parts along dimension 0
- d_w_up: bfloat16 [8192, 16384], P('groups', ('dp', 'expert')), parts along dimension 0
- d_w_down: bfloat16 [32768, 4096], P(('groups', 'dp', 'expert')), parts along dimension 0
There are 2 independent parts, one for each index of `groups`. A program takes and returns all parts, laid end to end along the dimension named above; each array names one. Nothing has to cross between parts.
Inputs may be any that keep to these rules, and one draw needn't show every extreme that they name: `slot_token`: no token fills two slots. The tokens of one device fill at most 6 slots together, and those of some device exactly 6.
All inputs are finite; a program needn't handle non-finite values.
Results may differ from a plain program's by a relative error of at most 0.024.
Values may be sent and summed in bfloat16 or wider, within the bound.
A program may use at most 128 MiB of HBM per device.

v0:
```python
import jax
import jax.numpy as jnp
from jax import lax
from jax.sharding import PartitionSpec as P

balance_weight = 2.0
zloss_weight = 0.3


def project_back(gate_rows, up_rows, w_gate, w_up):
    dims = (((1,), (1,)), ((), ()))
    first_part = lax.dot_general(gate_rows, w_gate, dims, preferred_element_type=jnp.float32)
    return first_part + lax.dot_general(up_rows, w_up, dims, preferred_element_type=jnp.float32)


def local(tokens, cotangent, router_weight, w_gate, w_up, w_down, slot_token):
    tok_dev = tokens.shape[0]
    expert_count = router_weight.shape[1]
    owner_count = lax.axis_size(("dp", "expert"))
    my_index = lax.axis_index(("dp", "expert"))
    slot_count = slot_token.shape[0]
    most_rows = 3 * tok_dev // 64
    over_rows = (((0,), (0,)), ((), ()))
    logits = jnp.dot(tokens, router_weight, preferred_element_type=jnp.float32)
    router_probs = jax.nn.softmax(logits, axis=-1)
    log_total = jax.nn.logsumexp(logits, axis=-1)
    column_sums = jnp.sum(router_probs, axis=0)
    load_total = lax.psum(column_sums, ("dp", "expert"))
    owner_dev = slot_token // tok_dev
    local_row = slot_token - owner_dev * tok_dev
    slot_order = jnp.arange(slot_count, dtype=jnp.int32)
    earlier = (owner_dev[None, :] == owner_dev[:, None]) & (
        slot_order[None, :] < slot_order[:, None]
    )
    rank_in = jnp.sum(earlier.astype(jnp.int32), axis=1)
    bucket_row = owner_dev * most_rows + rank_in
    bucket_hit = (owner_dev[None, :] == my_index) & (
        rank_in[None, :] == jnp.arange(most_rows, dtype=jnp.int32)[:, None]
    )
    filled = jnp.any(bucket_hit, axis=1)
    picked = jnp.sum(jnp.where(bucket_hit, local_row[None, :], 0), axis=1)
    my_slot = jnp.sum(jnp.where(bucket_hit, slot_order[None, :], 0), axis=1)
    send_tokens = jnp.where(filled[:, None], tokens[picked], jnp.zeros((), jnp.bfloat16))
    send_cot = jnp.where(filled[:, None], cotangent[picked], jnp.zeros((), jnp.bfloat16))
    send_gate = jnp.where(filled, router_probs[picked, 0], 0.0)
    all_tokens, all_cot, all_gate = (
        lax.all_gather(send_tokens, ("dp", "expert"), axis=0, tiled=True),
        lax.all_gather(send_cot, ("dp", "expert"), axis=0, tiled=True),
        lax.all_gather(send_gate.astype(jnp.bfloat16), ("dp", "expert"), axis=0, tiled=True).astype(
            send_gate.dtype
        ),
    )
    chosen = all_tokens[bucket_row]
    chosen_cot = all_cot[bucket_row]
    gate = all_gate[bucket_row]
    gate_pre = jnp.dot(chosen, w_gate, preferred_element_type=jnp.float32)
    up_pre = jnp.dot(chosen, w_up, preferred_element_type=jnp.float32)
    squash = jax.nn.sigmoid(gate_pre)
    swish = gate_pre * squash
    hidden = (swish * up_pre).astype(jnp.bfloat16)
    down_back = lax.dot_general(
        chosen_cot, w_down, (((1,), (1,)), ((), ())), preferred_element_type=jnp.float32
    )
    gate_part = jnp.sum(hidden.astype(jnp.float32) * down_back, axis=1)
    scaled_cot = (gate[:, None] * chosen_cot.astype(jnp.float32)).astype(jnp.bfloat16)
    d_w_down = lax.dot_general(
        hidden, scaled_cot, over_rows, preferred_element_type=jnp.float32
    ).astype(jnp.bfloat16)
    hidden_grad = gate[:, None] * down_back
    gate_back = (hidden_grad * up_pre * squash * (1.0 + gate_pre * (1.0 - squash))).astype(
        jnp.bfloat16
    )
    up_back = (hidden_grad * swish).astype(jnp.bfloat16)
    d_w_gate = lax.dot_general(
        chosen, gate_back, over_rows, preferred_element_type=jnp.float32
    ).astype(jnp.bfloat16)
    d_w_up = lax.dot_general(chosen, up_back, over_rows, preferred_element_type=jnp.float32).astype(
        jnp.bfloat16
    )
    slot_of = (
        jnp.full((owner_count * most_rows,), slot_count, jnp.int32).at[bucket_row].set(slot_order)
    )
    spare_row = jnp.zeros((1, gate_back.shape[1]), jnp.bfloat16)
    gate_rows = jnp.concatenate([gate_back, spare_row], axis=0)[slot_of]
    up_rows = jnp.concatenate([up_back, spare_row], axis=0)[slot_of]
    returned = lax.psum_scatter(
        project_back(gate_rows, up_rows, w_gate, w_up),
        ("dp", "expert"),
        scatter_dimension=0,
        tiled=True,
    ).astype(jnp.bfloat16)
    gate_total = lax.psum(gate_part, ("dp", "expert"))
    mean_load = load_total / (tok_dev * owner_count)
    bucket_gate = jnp.where(filled, gate_total[my_slot], 0.0)
    scatter_map = (picked[None, :] == jnp.arange(tok_dev, dtype=jnp.int32)[:, None]) & filled[
        None, :
    ]
    token_gate = jnp.sum(jnp.where(scatter_map, bucket_gate[None, :], 0.0), axis=1)
    first_column = (jnp.arange(expert_count) == 0).astype(jnp.float32)
    prob_grad = (
        2.0 * balance_weight * expert_count * mean_load[None, :]
        + token_gate[:, None] * first_column[None, :]
    )
    inner_sum = jnp.sum(router_probs * prob_grad, axis=1, keepdims=True)
    logit_grad = (
        router_probs * (prob_grad - inner_sum)
        + 2.0 * zloss_weight * log_total[:, None] * router_probs
    )
    logit_grad = logit_grad.astype(jnp.bfloat16)
    router_part = lax.dot_general(tokens, logit_grad, over_rows, preferred_element_type=jnp.float32)
    d_router = lax.psum(router_part, ("dp", "expert"))
    routed = jnp.dot(scatter_map.astype(jnp.bfloat16), returned, preferred_element_type=jnp.float32)
    through_router = lax.dot_general(
        logit_grad, router_weight, (((1,), (1,)), ((), ())), preferred_element_type=jnp.float32
    )
    d_tokens = (routed + through_router).astype(jnp.bfloat16)
    return (d_tokens, d_router, d_w_gate, d_w_up, d_w_down)


def solution(mesh):
    placed = (
        P(("groups", "dp", "expert"), None),
        P(("groups", "dp", "expert"), None),
        P("groups", None),
        P("groups", ("dp", "expert")),
        P("groups", ("dp", "expert")),
        P(("groups", "dp", "expert"), None),
        P("groups"),
    )
    return jax.shard_map(
        local,
        mesh=mesh,
        in_specs=placed,
        out_specs=(
            P(("groups", "dp", "expert"), None),
            P("groups", None),
            P("groups", ("dp", "expert")),
            P("groups", ("dp", "expert")),
            P(("groups", "dp", "expert"), None),
        ),
        check_vma=False,
    )
```

profile of v0, /device:TPU:0, one launch (start us, length us, event | category | flops | bytes accessed | tf_op | source)
XLA Modules:
  0.0 306.2 jit_solution(15509701983454826014)
XLA Ops:
  7.2 0.0 all-reduce.9.cloned.1.call-start
  7.2 0.7 multiply_subtract_fusion
  8.0 0.2 convert_reduce_fusion
  8.2 0.8 scatter_custom_fusion
  9.0 0.1 fusion.9
  9.1 0.1 select_reduce_fusion.1
  9.3 1.5 fusion.23
  10.9 0.1 fusion.19
  11.0 1.3 fusion.22
  13.0 0.7 gather_fusion
  13.7 0.2 dynamic-update-slice
  13.9 34.9 %all-reduce.3 = bf16[96]{0:T(256)(128)(2,1)S(1)} all-reduce(bf16[96]{0:T(256)(128)(2,1)S(1)} %dynamic-update-slice), channel_id=1, replica_groups=mesh['groups'=2,'dp'=4,'expert'=4] {'dp','expert'}, use_global_device_ids=true, to_apply=%add.3 | all-reduce | flops 96 | bytes 384
  48.8 0.6 gather_fusion.4
  49.4 2.0 gather_fusion.2
  51.4 0.1 select_bitcast_fusion
  51.5 21.3 %all-gather.1 = bf16[16,6,4096]{2,1,0:T(8,128)(2,1)S(1)} all-gather(bf16[1,6,4096]{2,1,0:T(8,128)(2,1)S(1)} %get-tuple-element.26), channel_id=1, replica_groups=mesh['groups'=2,'dp'=4,'expert'=4] {'dp','expert'}, dimensions={0}, use_global_device_ids=true | all-gather | bytes 835584 | tf_op jit(solution)/shard_map/all_gather | solution.py:47
  72.8 0.3 reshape.165
  73.1 0.8 gather_fusion.1
  73.9 0.9 gather_fusion.5
  74.8 5.7 %fusion.25 = f32[64,1024]{1,0:T(8,128)} fusion(bf16[64,4096]{1,0:T(8,128)(2,1)S(1)} %gather_fusion.5, bf16[4096,1024]{1,0:T(8,128)(2,1)} %param.10), kind=kOutput, calls=%fused_computation.80 | convolution fusion | flops 536870912 | bytes 9175040 | tf_op jit(solution)/shard_map/dot_general | solution.py:56
  80.4 5.7 %fusion.24 = f32[64,1024]{1,0:T(8,128)} fusion(bf16[64,4096]{1,0:T(8,128)(2,1)S(1)} %gather_fusion.5, bf16[4096,1024]{1,0:T(8,128)(2,1)} %param.11), kind=kOutput, calls=%fused_computation.79 | convolution fusion | flops 536870912 | bytes 9175040 | tf_op jit(solution)/shard_map/dot_general | solution.py:57
  86.1 21.3 %all-gather = bf16[16,6,4096]{2,1,0:T(8,128)(2,1)S(1)} all-gather(bf16[1,6,4096]{2,1,0:T(8,128)(2,1)S(1)} %get-tuple-element.27), channel_id=1, replica_groups=mesh['groups'=2,'dp'=4,'expert'=4] {'dp','expert'}, dimensions={0}, use_global_device_ids=true | all-gather | bytes 835584 | tf_op jit(solution)/shard_map/all_gather | solution.py:48
  107.3 0.3 reshape.163
  107.6 0.9 gather_fusion.3
  108.5 7.0 %multiply_reduce_fusion = (f32[64]{0:T(128)S(1)}, bf16[64,1024]{1,0:T(8,128)(2,1)}, bf16[64,1024]{1,0:T(8,128)(2,1)S(1)}, bf16[64,1024]{1,0:T(8,128)(2,1)S(1)}) fusion(f32[64,1024]{1,0:T(8,128)} %fusion.24, f32[64,1024]{1,0:T(8,128)} %fusion.25, f32[64]{0:T(128)S(1)} %gather_fusion.1, bf16[64,4096]{1,0:T(8,128)(2,1)S(1)} %gather_fusion.3, ...), kind=kOutput, calls=%fused_computation.19 | convolution fusion | flops 538116032 | bytes 9830912 | tf_op jit(solution)/shard_map/dot_general | solution.py:61
  115.5 0.8 gather_fusion.6
  116.3 1.5 gather_fusion.7
  117.8 6.1 %fusion.26 = f32[96,4096]{1,0:T(8,128)S(1)} fusion(bf16[96,1024]{1,0:T(8,128)(2,1)S(1)} %gather_fusion.6, bf16[4096,1024]{1,0:T(8,128)(2,1)} %param.10), kind=kOutput, calls=%fused_computation.81 | convolution fusion | flops 805306368 | bytes 10158080 | tf_op jit(solution)/shard_map/dot_general | solution.py:12
  123.9 6.1 %convolution_add_fusion.1 = f32[96,4096]{1,0:T(8,128)S(1)} fusion(f32[96,4096]{1,0:T(8,128)S(1)} %fusion.26, bf16[96,1024]{1,0:T(8,128)(2,1)S(1)} %copy-done.6, bf16[4096,1024]{1,0:T(8,128)(2,1)} %param.11), kind=kOutput, calls=%fused_computation.15 | convolution fusion | flops 805699584 | bytes 11730944 | tf_op jit(solution)/shard_map/dot_general | solution.py:13
  130.0 39.0 %fusion = f32[8,4096]{1,0:T(8,128)S(1)} fusion(f32[96,4096]{1,0:T(8,128)S(1)} %convolution_add_fusion.1), kind=kCustom, calls=%all-reduce-scatter | all-reduce-scatter fusion | flops 524289 | bytes 1704448
  169.1 1.9 collective-permute-start.1
  171.0 1.9 collective-permute-start.2
  172.9 1.9 collective-permute-start
  174.8 29.5 %all-reduce.6 = (f32[64]{0:T(128)S(1)}, f32[64]{0:T(128)S(1)}) all-reduce(f32[64]{0:T(128)S(1)} %get-tuple-element.13, f32[64]{0:T(128)S(1)} %get-tuple-element.11), channel_id=1, replica_groups=mesh['groups'=2,'dp'=4,'expert'=4] {'dp','expert'}, use_global_device_ids=true, to_apply=%region_10.11 | all-reduce | flops 128 | bytes 1024 | tf_op jit(solution)/shard_map/psum | solution.py:92
  204.3 0.6 gather_fusion.8
  205.0 0.1 select_reduce_fusion
  205.0 0.1 multiply_reduce_fusion.1
  205.1 1.3 convolution_bitcast_fusion
  206.5 0.6 slice.18
  207.1 1.9 collective-permute-start.3
  209.0 6.7 %convolution_convert_fusion.1 = bf16[4096,1024]{1,0:T(8,128)(2,1)} fusion(bf16[64,4096]{1,0:T(8,128)(2,1)S(1)} %gather_fusion.5, bf16[64,1024]{1,0:T(8,128)(2,1)} %copy-done.4), kind=kOutput, calls=%fused_computation.11 | convolution fusion | flops 541065216 | bytes 9043968 | tf_op jit(solution)/shard_map/dot_general | solution.py:77
  215.7 5.8 %convolution_convert_fusion.2 = bf16[4096,1024]{1,0:T(8,128)(2,1)} fusion(bf16[64,4096]{1,0:T(8,128)(2,1)S(1)} %gather_fusion.5, bf16[64,1024]{1,0:T(8,128)(2,1)S(1)} %get-tuple-element.17), kind=kOutput, calls=%fused_computation.12 | convolution fusion | flops 541065216 | bytes 9043968 | tf_op jit(solution)/shard_map/dot_general | solution.py:74
  221.5 5.8 %convolution_convert_fusion = bf16[1024,4096]{1,0:T(8,128)(2,1)} fusion(bf16[64,1024]{1,0:T(8,128)(2,1)S(1)} %copy-done.5, bf16[64,4096]{1,0:T(8,128)(2,1)S(1)} %copy-done.2, f32[64]{0:T(128)S(1)} %gather_fusion.1), kind=kOutput, calls=%fused_computation.10 | convolution fusion | flops 541851648 | bytes 9044224 | tf_op jit(solution)/shard_map/dot_general | solution.py:66
  227.3 0.5 fusion.18
  228.4 7.9 %concatenate.14 = bf16[38,4096]{1,0:T(8,128)(2,1)} concatenate(bf16[6,4096]{1,0:T(8,128)(2,1)} %collective-permute-done.3, bf16[8,4096]{1,0:T(8,128)(2,1)} %collective-permute-done.2, bf16[8,4096]{1,0:T(8,128)(2,1)} %collective-permute-done.1, bf16[8,4096]{1,0:T(8,128)(2,1)} %collective-permute-done, f32[8,4096]{1,0:T(8,128)S(1)} %fusion), dimensions={0} | concatenate | bytes 688128
  236.4 2.4 fusion.1
  238.8 58.2 %all-reduce.9.cloned.1.call-done = f32[4096,64]{0,1:T(8,128)} async-done(((f32[4096,64]{0,1:T(8,128)}), f32[4096,64]{0,1:T(8,128)}) %all-reduce.9.cloned.1.call-update) | async-done | bytes 1048592 | tf_op jit(solution)/shard_map/psum | solution.py:111
  297.1 2.3 copy.14
  (41 shorter events, 0.2 us)
Async XLA Ops:
  7.2 2.2 copy-start
  7.2 289.9 %all-reduce.9.cloned.1.call-start = ((), (), s32[]{:S(2)}) async-start(), calls=%async_computation | async-start | bytes 2097152 | tf_op jit(solution)/shard_map/psum | solution.py:111
  108.5 9.3 %copy-start.1 = (bf16[64,4096]{1,0:T(8,128)(2,1)}, bf16[64,4096]{1,0:T(8,128)(2,1)S(1)}, u32[]{:S(2)}) copy-start(bf16[64,4096]{1,0:T(8,128)(2,1)S(1)} %gather_fusion.3) | copy-start | bytes 1572868
  115.5 2.3 copy-start.4
  117.8 6.1 %copy-start.6 = (bf16[96,1024]{1,0:T(8,128)(2,1)S(1)}, bf16[96,1024]{1,0:T(8,128)(2,1)}, u32[]{:S(2)}) copy-start(bf16[96,1024]{1,0:T(8,128)(2,1)} %gather_fusion.7) | copy-start | bytes 589828
  169.1 59.3 %collective-permute-start.1 = (bf16[8,4096]{1,0:T(8,128)(2,1)S(1)}, bf16[8,4096]{1,0:T(8,128)(2,1)}, u32[]{:S(2)}, u32[]{:S(2)}) collective-permute-start(bf16[8,4096]{1,0:T(8,128)(2,1)S(1)} %convert.14), channel_id=1, source_target_pairs={{0,2},{1,3},{2,4},{3,5},{4,6},{5,7},{6,8},{7,9},{8,10},{9,11},{10,... | collective-permute-start | bytes 196616
  171.0 57.4 %collective-permute-start.2 = (bf16[8,4096]{1,0:T(8,128)(2,1)S(1)}, bf16[8,4096]{1,0:T(8,128)(2,1)}, u32[]{:S(2)}, u32[]{:S(2)}) collective-permute-start(bf16[8,4096]{1,0:T(8,128)(2,1)S(1)} %convert.14), channel_id=1, source_target_pairs={{0,3},{1,4},{2,5},{3,6},{4,7},{5,8},{6,9},{7,10},{8,11},{9,12},{10... | collective-permute-start | bytes 196616
  172.9 55.6 %collective-permute-start = (bf16[8,4096]{1,0:T(8,128)(2,1)S(1)}, bf16[8,4096]{1,0:T(8,128)(2,1)}, u32[]{:S(2)}, u32[]{:S(2)}) collective-permute-start(bf16[8,4096]{1,0:T(8,128)(2,1)S(1)} %convert.14), channel_id=1, source_target_pairs={{0,1},{1,2},{2,3},{3,4},{4,5},{5,6},{6,7},{7,8},{8,9},{9,10},{10,1... | collective-permute-start | bytes 196616
  207.1 21.3 %collective-permute-start.3 = (bf16[6,4096]{1,0:T(8,128)(2,1)}, bf16[6,4096]{1,0:T(8,128)(2,1)}, u32[]{:S(2)}, u32[]{:S(2)}) collective-permute-start(bf16[6,4096]{1,0:T(8,128)(2,1)} %slice.18), channel_id=1, source_target_pairs={{0,4},{1,5},{2,6},{3,7},{4,8},{5,9},{6,10},{7,11},{8,12},{9,13},{1... | collective-permute-start | bytes 147464
  215.7 5.8 %copy-start.2 = (bf16[64,4096]{1,0:T(8,128)(2,1)S(1)}, bf16[64,4096]{1,0:T(8,128)(2,1)}, u32[]{:S(2)}) copy-start(bf16[64,4096]{1,0:T(8,128)(2,1)} %copy-done.1) | copy-start | bytes 1572868
  215.7 5.8 %copy-start.5 = (bf16[64,1024]{1,0:T(8,128)(2,1)S(1)}, bf16[64,1024]{1,0:T(8,128)(2,1)}, u32[]{:S(2)}) copy-start(bf16[64,1024]{1,0:T(8,128)(2,1)} %get-tuple-element.14) | copy-start | bytes 393220
  221.5 5.8 %copy-start.3 = (bf16[4096,64]{0,1:T(8,128)(2,1)S(1)}, bf16[4096,64]{0,1:T(8,128)(2,1)}, u32[]{:S(2)}) copy-start(bf16[4096,64]{0,1:T(8,128)(2,1)} %param.9) | copy-start | bytes 1572868
Sparse Core Ops, SparseCore 0:
  206.6 90.4 all-reduce.8
where the time goes:
time: 307 us; the launch traced here: 306 us
  blocking collectives  146 us (48%)
  waiting for transfers between devices  58.3 us (19%)
  matrix products  54.6 us (18%)
  local copies, waits for them, and re-layouts  22.4 us (7%)
  between operations  15.5 us (5%)
  starting transfers between devices  7.65 us (2%)
    unnamed x2, blocking collectives  73.9 us
    psum x1, waiting for transfers between devices, local(): d_router = lax.psum(router_part, ('dp', 'expert'))  58.2 us
    psum x1, blocking collectives, local(): gate_total = lax.psum(gate_part, ('dp', 'expert'))  29.5 us
    all_gather x1, blocking collectives, local(): lax.all_gather(send_tokens, ('dp', 'expert'), axis=0, tiled=True)  21.3 us
    all_gather x1, blocking collectives, local(): lax.all_gather(send_cot, ('dp', 'expert'), axis=0, tiled=True)  21.3 us
    unnamed x22, local copies, waits for them, and re-layouts  13 us
    unnamed x4, starting transfers between devices  7.61 us
    dot_general x1, matrix products, local(): lax.dot_general(chosen_cot, w_down, (((1,), (1,)), ((), ())), preferred_e...  7.01 us
  transfers between devices with their start and end apart: 5, of which 1 were waited for; matrix products, arithmetic and copies ran while one was open for 10% of the time, Pallas kernels for 0%

commit v1 on v0

--- a/solution.py
+++ b/solution.py
@@ -1,6 +1,10 @@
+import functools
+
 import jax
 import jax.numpy as jnp
 from jax import lax
+from jax.experimental import pallas as pl
+from jax.experimental.pallas import tpu as pltpu
 from jax.sharding import PartitionSpec as P
 
 balance_weight = 2.0
@@ -117,6 +121,472 @@
     return (d_tokens, d_router, d_w_gate, d_w_up, d_w_down)
 
 
+MESH = pl.DeviceIdType.MESH
+f32, bf16 = jnp.float32, jnp.bfloat16
+PAD = 8
+NT = (((1,), (1,)), ((), ()))
+TN = (((0,), (0,)), ((), ()))
+HI = lax.Precision.HIGHEST
+
+
+class Place:
+    def __init__(self, nd, ne):
+        self.nd, self.nx, self.n = nd, ne // 2, nd * ne
+        self.ne = ne
+        self.d = lax.axis_index("dp")
+        e = lax.axis_index("expert")
+        self.x, self.c = e // 2, e % 2
+        self.me = self.d * ne + e
+
+    def at(self, d, x, c):
+        return {"dp": d, "expert": 2 * x + c}
+
+    def peer(self, offset):
+        other = lax.rem(self.me + offset, self.n)
+        return other, {"dp": other // self.ne, "expert": lax.rem(other, self.ne)}
+
+
+def greet(place):
+    barrier = pltpu.get_barrier_semaphore()
+    for offset in range(1, place.n):
+        pl.semaphore_signal(barrier, inc=1, device_id=place.peer(offset)[1], device_id_type=MESH)
+    return barrier
+
+
+def to_all(place, buf, send_sem, recv_sem):
+    out = []
+    for offset in range(1, place.n):
+        _, where = place.peer(offset)
+        out.append(
+            pltpu.make_async_remote_copy(
+                buf.at[place.me], buf.at[place.me], send_sem.at[offset - 1], recv_sem.at[place.me],
+                device_id=where, device_id_type=MESH,
+            )
+        )
+    return out
+
+
+def from_all(place, buf, send_sem, recv_sem):
+    for offset in range(1, place.n):
+        other, where = place.peer(offset)
+        pltpu.make_async_remote_copy(
+            buf.at[other], buf.at[other], send_sem.at[offset - 1], recv_sem.at[other],
+            device_id=where, device_id_type=MESH,
+        ).wait_recv()
+
+
+def gather_blocks(place, buf, send_sem, recv_sem, mid=None):
+    d, x, c, nd = place.d, place.x, place.c, place.nd
+
+    def copy(kind, bd, bx, bc, where):
+        block = bd * place.ne + 2 * bx + bc
+        return pltpu.make_async_remote_copy(
+            buf.at[block], buf.at[block], send_sem.at[kind, block], recv_sem.at[block],
+            device_id=where, device_id_type=MESH,
+        )
+
+    up = lambda bd: copy(0, bd, x, c, place.at(d + 1, x, c))
+    down = lambda bd: copy(0, bd, x, c, place.at(d - 1, x, c))
+    across = lambda bd: copy(1, bd, x, c, place.at(d, 1 - x, c))
+    sibling = lambda bd, bx: copy(2, bd, bx, c, place.at(d, x, 1 - c))
+    up_own = copy(3, d, x, c, place.at(d + 1, x, c))
+
+    @pl.when(d < nd - 1)
+    def _():
+        up_own.start()
+
+    @pl.when(d > 0)
+    def _():
+        down(d).start()
+
+    across(d).start()
+    sibling(d, x).start()
+    if mid is not None:
+        mid()
+
+    def arrived(bd, bx, bc):
+        copy(0, bd, bx, bc, place.at(d, x, 1 - c)).wait_recv()
+
+    for step in range(1, nd + 1):
+        if step < nd:
+            low, high = d - step, d + step
+
+            @pl.when(low >= 0)
+            def _():
+                arrived(low, x, c)
+
+                @pl.when(d < nd - 1)
+                def _():
+                    up(low).start()
+
+                across(low).start()
+                sibling(low, x).start()
+
+            @pl.when(high < nd)
+            def _():
+                arrived(high, x, c)
+
+                @pl.when(d > 0)
+                def _():
+                    down(high).start()
+
+                across(high).start()
+                sibling(high, x).start()
+
+        low, high = d - (step - 1), d + (step - 1)
+
+        @pl.when(low >= 0)
+        def _():
+            arrived(low, 1 - x, c)
+            sibling(low, 1 - x).start()
+
+        if step > 1:
+            @pl.when(high < nd)
+            def _():
+                arrived(high, 1 - x, c)
+                sibling(high, 1 - x).start()
+
+    for bd in range(nd):
+        for bx in range(place.nx):
+            arrived(bd, bx, 1 - c)
+
+    @pl.when(d < nd - 1)
+    def _():
+        up_own.wait_send()
+
+    @pl.when(d > 0)
+    def _():
+        down(d).wait_send()
+
+    for bd in range(nd):
+        @pl.when((bd < d) & (d < nd - 1))
+        def _():
+            up(bd).wait_send()
+
+        @pl.when((bd > d) & (d > 0))
+        def _():
+            down(bd).wait_send()
+
+        across(bd).wait_send()
+        for bx in range(place.nx):
+            sibling(bd, bx).wait_send()
+
+
+def own_slots(slot_row, slot_col, me, tok_dev, row_start, rows):
+    slots = slot_row.shape[1]
+    local_row = slot_row - me * tok_dev
+    hit = ((local_row >= 0) & (local_row < tok_dev)).astype(f32)
+    before = (
+        lax.broadcasted_iota(jnp.int32, (slots, slots), 0)
+        < lax.broadcasted_iota(jnp.int32, (slots, slots), 1)
+    ).astype(f32).astype(bf16)
+    rank = jnp.dot(jnp.broadcast_to(hit, (8, slots)).astype(bf16), before, preferred_element_type=f32)[:1]
+    wanted = (lax.broadcasted_iota(jnp.int32, (rows, slots), 0) - row_start).astype(f32)
+    take = jnp.where(wanted == rank, hit, 0.0)
+    holds = (lax.broadcasted_iota(jnp.int32, (slots, tok_dev), 1) == slot_col - me * tok_dev).astype(f32)
+    return take.astype(bf16), holds.astype(bf16)
+
+
+def gather_kernel(nd, ne, tok, cot, rw, slot_row, slot_col, rows, probs_out, log_out, load_out,
+                  loads, send_sem, recv_sem, load_send, load_recv):
+    place = Place(nd, ne)
+    barrier = greet(place)
+    tok_dev = tok.shape[0]
+    take, holds = own_slots(slot_row[...], slot_col[...], place.me, tok_dev, 0, PAD)
+    pick = jnp.dot(take, holds, preferred_element_type=f32).astype(bf16)
+    width = tok.shape[1] // 4
+    for part in range(4):
+        cols = pl.ds(part * width, width)
+        both = jnp.concatenate(
+            [jnp.dot(pick, tok[:, cols], preferred_element_type=f32),
+             jnp.dot(pick, cot[:, cols], preferred_element_type=f32)], axis=0)
+        rows[place.me, :, cols] = both.astype(bf16)
+    pl.semaphore_wait(barrier, place.n - 1)
+    sends = to_all(place, loads, load_send, load_recv)
+
+    def mid():
+        logits = jnp.dot(tok[...], rw[...], preferred_element_type=f32)
+        top = jnp.max(logits, axis=1, keepdims=True)
+        raised = jnp.exp(logits - top)
+        total = jnp.sum(raised, axis=1, keepdims=True)
+        probs = raised / total
+        probs_out[...] = probs
+        log_out[...] = jnp.log(total) + top
+        loads[place.me] = jnp.broadcast_to(jnp.sum(probs, axis=0, keepdims=True), loads.shape[1:])
+        for send in sends:
+            send.start()
+
+    gather_blocks(place, rows, send_sem, recv_sem, mid)
+    from_all(place, loads, load_send, load_recv)
+    for send in sends:
+        send.wait_send()
+    load_out[...] = jnp.sum(loads[...], axis=0)
+
+
+def expert_kernel(steps, nd, ne, rows, rw, wg, wu, wd, dwg, dwu, dwd, sums, gate_out,
+                  ch, cht, ct, sc, gate, acc, part):
+    step = pl.program_id(0)
+    owners = nd * ne
+    slots = owners * PAD
+    width = rows.shape[2]
+
+    @pl.when(step == 0)
+    def _():
+        for pair in range(owners // 2):
+            first, second = rows[2 * pair].astype(f32), rows[2 * pair + 1].astype(f32)
+            span = pl.ds(pair * 2 * PAD, 2 * PAD)
+            ch[span, :] = jnp.concatenate([first[:PAD], second[:PAD]], axis=0).astype(bf16)
+            ct[span, :] = jnp.concatenate([first[PAD:], second[PAD:]], axis=0).astype(bf16)
+        for k in range(width // 512):
+            cht[pl.ds(k * 512, 512), :] = ch[:, pl.ds(k * 512, 512)].T
+        logits = jnp.dot(ch[...], rw[...], preferred_element_type=f32)
+        raised = jnp.exp(logits - jnp.max(logits, axis=1, keepdims=True))
+        probs = raised / jnp.sum(raised, axis=1, keepdims=True)
+        gate[...] = probs[:, :1]
+        for k in range(width // 512):
+            cols = pl.ds(k * 512, 512)
+            sc[:, cols] = (gate[...] * ct[:, cols].astype(f32)).astype(bf16)
+        acc[...] = jnp.zeros_like(acc)
+        part[...] = jnp.zeros_like(part)
+
+    gate_pre = jnp.dot(ch[...], wg[...], preferred_element_type=f32)
+    up_pre = jnp.dot(ch[...], wu[...], preferred_element_type=f32)
+    down_back = lax.dot_general(ct[...], wd[...], NT, preferred_element_type=f32)
+    squash = jax.nn.sigmoid(gate_pre)
+    swish = gate_pre * squash
+    hidden = (swish * up_pre).astype(bf16)
+    part[...] += jnp.sum(hidden.astype(f32) * down_back, axis=1, keepdims=True)
+    hidden_grad = gate[...] * down_back
+    gate_back = (hidden_grad * up_pre * squash * (1.0 + gate_pre * (1.0 - squash))).astype(bf16)
+    up_back = (hidden_grad * swish).astype(bf16)
+    hidden_t = hidden.T
+    for k in range(width // 512):
+        span = pl.ds(k * 512, 512)
+        dwd[:, span] = jnp.dot(hidden_t, sc[:, span], preferred_element_type=f32).astype(bf16)
+        dwg[span, :] = jnp.dot(cht[span, :], gate_back, preferred_element_type=f32).astype(bf16)
+        dwu[span, :] = jnp.dot(cht[span, :], up_back, preferred_element_type=f32).astype(bf16)
+        acc[:, span] += lax.dot_general(
+            gate_back, wg[span, :], NT, preferred_element_type=f32
+        ) + lax.dot_general(up_back, wu[span, :], NT, preferred_element_type=f32)
+
+    @pl.when(step == steps - 1)
+    def _():
+        for owner in range(owners):
+            dd, e = owner // ne, owner % ne
+            for k in range(width // 512):
+                pair = jnp.concatenate(
+                    [acc[pl.ds(owner * PAD, PAD), pl.ds(512 * k, 256)],
+                     acc[pl.ds(owner * PAD, PAD), pl.ds(512 * k + 256, 256)]], axis=0)
+                sums[e % 2, e // 2, dd, pl.ds(16 * k, 16), :] = pair.astype(bf16)
+        gate_out[...] = jnp.broadcast_to(part[...], (slots, slots)).T[:8]
+
+
+class Scatter:
+    def __init__(self, place, src, from_core, one, from_x, two, from_z, sems):
+        self.p, self.src = place, src
+        self.from_core, self.one, self.from_x, self.two, self.from_z = from_core, one, from_x, two, from_z
+        self.cs, self.cr, self.xs, self.xr, self.zs, self.zr = sems
+        p = place
+        self.core = [
+            pltpu.make_async_remote_copy(
+                src.at[1 - p.c, bx], from_core.at[bx], self.cs.at[bx], self.cr.at[bx],
+                device_id=p.at(p.d, p.x, 1 - p.c), device_id_type=MESH)
+            for bx in (1 - p.x, p.x)
+        ]
+        self.across = [
+            pltpu.make_async_remote_copy(
+                one.at[bd], from_x.at[bd], self.xs.at[bd], self.xr.at[bd],
+                device_id=p.at(p.d, 1 - p.x, p.c), device_id_type=MESH)
+            for bd in range(p.nd)
+        ]
+
+    def start_core(self):
+        for send in self.core:
+            send.start()
+
+    def start_across(self):
+        p = self.p
+        self.core_in(1 - p.x)
+        for bd in range(p.nd):
+            self.one[bd] = (
+                self.src[p.c, 1 - p.x, bd].astype(f32) + self.from_core[1 - p.x, bd].astype(f32)
+            ).astype(self.one.dtype)
+            self.across[bd].start()
+        self.core_in(p.x)
+
+    def core_in(self, bx):
+        p = self.p
+        pltpu.make_async_remote_copy(
+            self.src.at[1 - p.c, bx], self.from_core.at[bx], self.cs.at[bx], self.cr.at[bx],
+            device_id=p.at(p.d, p.x, 1 - p.c), device_id_type=MESH).wait_recv()
+
+    def along(self, bd, slot):
+        p = self.p
+        return pltpu.make_async_remote_copy(
+            self.two.at[bd], self.from_z.at[slot], self.zs.at[bd], self.zr.at[slot],
+            device_id=p.at(bd, p.x, p.c), device_id_type=MESH)
+
+    def start_along(self):
+        p = self.p
+        for bd in range(p.nd):
+            self.across[bd].wait_recv()
+            self.two[bd] = (
+                self.src[p.c, p.x, bd].astype(f32) + self.from_core[p.x, bd].astype(f32)
+                + self.from_x[bd].astype(f32)
+            ).astype(self.two.dtype)
+
+            @pl.when(p.d != bd)
+            def _():
+                self.along(bd, p.d).start()
+
+    def finish(self):
+        p = self.p
+        self.from_z[p.d] = self.two[p.d]
+        for bd in range(p.nd):
+            @pl.when(p.d != bd)
+            def _():
+                self.along(bd, bd).wait_recv()
+        total = self.from_z[0].astype(f32)
+        for bd in range(1, p.nd):
+            total = total + self.from_z[bd].astype(f32)
+        return total
+
+    def drain(self):
+        p = self.p
+        for send in self.core + self.across:
+            send.wait_send()
+        for bd in range(p.nd):
+            @pl.when(p.d != bd)
+            def _():
+                self.along(bd, p.d).wait_send()
+
+
+def combine_kernel(nd, ne, sums, gate_part, tok, rw, probs_in, log_in, load_in, slot_row, slot_col,
+                   d_tok, d_rout, gates, rpart, s_core, s_one, s_x, s_two, s_z,
+                   r_core, r_one, r_x, r_two, r_z, gate_send, gate_recv,
+                   a0, a1, a2, a3, a4, a5, b0, b1, b2, b3, b4, b5, g_send, g_recv):
+    place = Place(nd, ne)
+    barrier = greet(place)
+    me = place.me
+    tok_dev, experts = probs_in.shape
+    slots = gate_part.shape[1]
+    gates[me] = gate_part[...]
+    take, holds = own_slots(slot_row[...], slot_col[...], me, tok_dev, 0, PAD)
+    take_all, _ = own_slots(slot_row[...], slot_col[...], me, tok_dev, me * PAD, slots)
+    tn = (((0,), (1,)), ((), ()))
+    place_own = lax.dot_general(holds, take, tn, preferred_element_type=f32).astype(bf16)
+    place_all = lax.dot_general(holds, take_all, tn, preferred_element_type=f32)
+    pl.semaphore_wait(barrier, place.n - 1)
+    rows = Scatter(place, sums, s_core, s_one, s_x, s_two, s_z, (a0, a1, a2, a3, a4, a5))
+    rout = Scatter(place, rpart, r_core, r_one, r_x, r_two, r_z, (b0, b1, b2, b3, b4, b5))
+    gate_sends = to_all(place, gates, gate_send, gate_recv)
+    for send in gate_sends:
+        send.start()
+    rows.start_core()
+    rows.start_across()
+    from_all(place, gates, gate_send, gate_recv)
+    gate_total = jnp.sum(gates[...], axis=0)[:1]
+    token_gate = jnp.sum(place_all * gate_total, axis=1, keepdims=True)
+    probs = probs_in[...]
+    mean_load = load_in[:1] / (tok_dev * place.n)
+    first = (lax.broadcasted_iota(jnp.int32, (1, experts), 1) == 0).astype(f32)
+    prob_grad = 2.0 * balance_weight * experts * mean_load + token_gate * first
+    inner = jnp.sum(probs * prob_grad, axis=1, keepdims=True)
+    lg = probs * (prob_grad - inner) + 2.0 * zloss_weight * log_in[...] * probs
+    lg = lg.astype(bf16)
+    for owner in range(place.n):
+        dd, e = owner // ne, owner % ne
+        rpart[e % 2, e // 2, dd] = lax.dot_general(
+            lg, tok[:, pl.ds(256 * owner, 256)], TN, preferred_element_type=f32)
+    rout.start_core()
+    rout.start_across()
+    rows.start_along()
+    rout.start_along()
+    d_rout[me] = rout.finish().astype(bf16)
+
+    def mid():
+        returned = rows.finish().astype(bf16).astype(f32)
+        for k in range(tok.shape[1] // 256):
+            cols = pl.ds(256 * k, 256)
+            block = returned[PAD * k:PAD * (k + 1)].astype(bf16)
+            d_tok[:, cols] = (
+                jnp.dot(place_own, block, preferred_element_type=f32)
+                + lax.dot_general(lg, rw[cols, :], NT, preferred_element_type=f32)
+            ).astype(bf16)
+
+    gather_blocks(place, d_rout, g_send, g_recv, mid)
+    rows.drain()
+    rout.drain()
+    for send in gate_sends:
+        send.wait_send()
+
+
+def fast_local(nd, ne, tokens, cotangent, router_weight, w_gate, w_up, w_down, slot_token):
+    tok_dev, width = tokens.shape
+    experts = router_weight.shape[1]
+    ff = w_gate.shape[1]
+    owners = nd * ne
+    slots = owners * PAD
+    nx = ne // 2
+    slot_row, slot_col = slot_token[None, :], slot_token[:, None]
+    vmem = pl.BlockSpec(memory_space=pltpu.VMEM)
+    dma = pltpu.SemaphoreType.DMA
+    sds = jax.ShapeDtypeStruct
+    limit = 56 * 2**20
+    rows, probs, log_total, load = pl.pallas_call(
+        functools.partial(gather_kernel, nd, ne),
+        out_shape=(sds((owners, 2 * PAD, width), bf16), sds((tok_dev, experts), f32),
+                   sds((tok_dev, 1), f32), sds((8, experts), f32)),
+        in_specs=[vmem] * 5,
+        out_specs=(vmem,) * 4,
+        scratch_shapes=[pltpu.VMEM((owners, 8, experts), f32), dma((4, owners)), dma((owners,)),
+                        dma((owners - 1,)), dma((owners,))],
+        compiler_params=pltpu.CompilerParams(
+            collective_id=0, has_side_effects=True, vmem_limit_bytes=limit),
+    )(tokens, cotangent, router_weight, slot_row, slot_col)
+
+    tile = 256
+    steps = ff // tile
+    whole = lambda *shape: pl.BlockSpec(shape, lambda i: (0,) * len(shape))
+    columns = pl.BlockSpec((width, tile), lambda i: (0, i))
+    lines = pl.BlockSpec((tile, width), lambda i: (i, 0))
+    d_w_gate, d_w_up, d_w_down, sums, gate_part = pl.pallas_call(
+        functools.partial(expert_kernel, steps, nd, ne),
+        grid=(steps,),
+        out_shape=(sds(w_gate.shape, bf16), sds(w_up.shape, bf16), sds(w_down.shape, bf16),
+                   sds((2, nx, nd, PAD * width // 256, 256), bf16), sds((8, slots), f32)),
+        in_specs=[whole(owners, 2 * PAD, width), whole(width, experts), columns, columns, lines],
+        out_specs=(columns, columns, lines, whole(2, nx, nd, PAD * width // 256, 256), whole(8, slots)),
+        scratch_shapes=[pltpu.VMEM((slots, width), bf16), pltpu.VMEM((width, slots), bf16),
+                        pltpu.VMEM((slots, width), bf16), pltpu.VMEM((slots, width), bf16),
+                        pltpu.VMEM((slots, 1), f32), pltpu.VMEM((slots, width), f32),
+                        pltpu.VMEM((slots, 1), f32)],
+        compiler_params=pltpu.CompilerParams(vmem_limit_bytes=limit),
+    )(rows, router_weight, w_gate, w_up, w_down)
+
+    sblock, rblock = (PAD * width // 256, 256), (experts, 256)
+
+    def stages(block, kind):
+        return [pltpu.VMEM((nx, nd) + block, kind), pltpu.VMEM((nd,) + block, kind),
+                pltpu.VMEM((nd,) + block, kind), pltpu.VMEM((nd,) + block, kind),
+                pltpu.VMEM((nd,) + block, kind)]
+
+    stage_sems = [dma((nx,)), dma((nx,)), dma((nd,)), dma((nd,)), dma((nd,)), dma((nd,))]
+    d_tokens, d_rout = pl.pallas_call(
+        functools.partial(combine_kernel, nd, ne),
+        out_shape=(sds((tok_dev, width), bf16), sds((owners, experts, 256), bf16)),
+        in_specs=[vmem] * 9,
+        out_specs=(vmem,) * 2,
+        scratch_shapes=[pltpu.VMEM((owners, 8, slots), f32), pltpu.VMEM((2, nx, nd) + rblock, f32)]
+        + stages(sblock, bf16) + stages(rblock, f32) + [dma((owners - 1,)), dma((owners,))]
+        + stage_sems + stage_sems + [dma((4, owners)), dma((owners,))],
+        compiler_params=pltpu.CompilerParams(
+            collective_id=1, has_side_effects=True, vmem_limit_bytes=limit),
+    )(sums, gate_part, tokens, router_weight, probs, log_total, load, slot_row, slot_col)
+    d_router = jnp.transpose(d_rout, (0, 2, 1)).reshape(width, experts).astype(f32)
+    return d_tokens, d_router, d_w_gate, d_w_up, d_w_down
+
+
 def solution(mesh):
     placed = (
         P(("groups", "dp", "expert"), None),
@@ -127,8 +597,10 @@
         P(("groups", "dp", "expert"), None),
         P("groups"),
     )
+    nd, ne = mesh.shape["dp"], mesh.shape["expert"]
+    body = functools.partial(fast_local, nd, ne) if (nd, ne) == (4, 4) else local
     return jax.shard_map(
-        local,
+        body,
         mesh=mesh,
         in_specs=placed,
         out_specs=(

time: 307 us -> 106 us (0.35)
  blocking collectives: 146 us -> 0 us
  Pallas kernels: 0 us -> 97.1 us
  waiting for transfers between devices: 58.3 us -> 0 us
  matrix products: 54.6 us -> 0 us
  local copies, waits for them, and re-layouts: 22.4 us -> 7.07 us
  between operations: 15.5 us -> 0.66 us
  starting transfers between devices: 7.65 us -> 0 us
    pallas_call x0 -> x3, Pallas kernels: none -> 97.1 us  [the longest x1 41.4 us: fast_local(): pl.pallas_call(functools.partial(combine_kernel, nd, ne), out_shape=(sds(...]
    unnamed x2 -> x0, blocking collectives: 73.9 us -> none
    psum x1 -> x0, waiting for transfers between devices: 58.2 us -> none  [local(): d_router = lax.psum(router_part, ('dp', 'expert'))]
    dot_general x12 -> x0, matrix products: 54.6 us -> none  [the longest x1 7.01 us: local(): lax.dot_general(chosen_cot, w_down, (((1,), (1,)), ((), ())), preferred_e...]
    all_gather x2 -> x0, blocking collectives: 42.6 us -> none  [the longest x1 21.3 us: local(): lax.all_gather(send_tokens, ('dp', 'expert'), axis=0, tiled=True)]
    psum x1 -> x0, blocking collectives: 29.5 us -> none  [local(): gate_total = lax.psum(gate_part, ('dp', 'expert'))]
    gather x9 -> x0, local copies, waits for them, and re-layouts: 8.62 us -> none  [the longest x1 1.99 us: local(): cotangent[picked]]
    unnamed x22 -> x2, local copies, waits for them, and re-layouts: 13 us -> 4.64 us
  transfers between devices with their start and end apart: 5 -> 0, of which waited for: 1 -> 0; matrix products, arithmetic and copies ran while one was open for 10% -> 0% of each run, Pallas kernels for 0% -> 0%
where the time goes in v1:
time: 106 us
  Pallas kernels  97.1 us (92%)
  local copies, waits for them, and re-layouts  7.07 us (7%)
  other arithmetic  1.15 us (1%)
    pallas_call x1, Pallas kernels, fast_local(): pl.pallas_call(functools.partial(combine_kernel, nd, ne), out_shape=(sds(...  41.4 us
    pallas_call x1, Pallas kernels, fast_local(): pl.pallas_call(functools.partial(expert_kernel, steps, nd, ne), grid=(ste...  28.3 us
    pallas_call x1, Pallas kernels, fast_local(): pl.pallas_call(functools.partial(gather_kernel, nd, ne), out_shape=(sds((...  27.4 us
    unnamed x2, local copies, waits for them, and re-layouts  4.64 us

profile of v1, /device:TPU:0, one launch (start us, length us, event | category | flops | bytes accessed | tf_op | source)
XLA Modules:
  0.0 106.0 jit_solution(4507916946073044019)
XLA Ops:
  0.6 1.4 %copy.18.slot_col = s32[64,1]{1,0:T(8,128)} copy(s32[64,1]{0,1:T(1,128)} %bitcast.7) | data formatting | bytes 512 | tf_op jit(solution)/shard_map/broadcast_in_dim | solution.py:531
  2.0 2.4 %copy.17.rw = bf16[4096,64]{1,0:T(8,128)(2,1)} copy(bf16[4096,64]{0,1:T(8,128)(2,1)} %param.9) | data formatting | bytes 1048576 | tf_op args[2]
  4.3 27.4 %shard_map.110 = (bf16[16,16,4096]{2,1,0:T(8,128)(2,1)}, f32[128,64]{1,0:T(8,128)}, f32[128,1]{1,0:T(8,128)}, f32[8,64]{1,0:T(8,128)}) custom-call(bf16[128,4096]{1,0:T(8,128)(2,1)} %tok.3, bf16[128,4096]{1,0:T(8,128)(2,1)} %cot.1, bf16[4096,64]{1,0:T(8,128)(2,1)} %copy.17.rw, s32[1,64]{1,0:T(1,128)} %bitcast.8, s32[64,1]{1,0:T(8,128)} %copy.18.slot_col), custom_call_target="tpu_custom_call" | custom-call | tf_op jit(solution)/shard_map/pallas_call | solution.py:536
  31.7 28.3 %shard_map.111 = (bf16[4096,1024]{1,0:T(8,128)(2,1)}, bf16[4096,1024]{1,0:T(8,128)(2,1)}, bf16[1024,4096]{1,0:T(8,128)(2,1)}, bf16[2,2,4,128,256]{4,3,2,1,0:T(8,128)(2,1)}, f32[8,128]{1,0:T(8,128)}) custom-call(bf16[16,16,4096]{2,1,0:T(8,128)(2,1)} %get-tuple-element.16.rows, bf16[4096,64]{1,0:T(8,128)(2,1)} %copy.17.rw, bf16[4096,1024]{1,0:T(8,128)(2,1)} %wg.1, ...), custom_call_target="tpu_custom_call" | custom-call | tf_op jit(solution)/shard_map/pallas_call | solution.py:553
  60.1 41.4 %shard_map.112 = (bf16[128,4096]{1,0:T(8,128)(2,1)}, bf16[16,64,256]{2,1,0:T(8,128)(2,1)}) custom-call(bf16[2,2,4,128,256]{4,3,2,1,0:T(8,128)(2,1)} %get-tuple-element.17.sums, f32[8,128]{1,0:T(8,128)} %get-tuple-element.18.gate_part, bf16[128,4096]{1,0:T(8,128)(2,1)} %tok.3, bf16[4096,64]{1,0:T(8,128)(2,1)} %copy.17.rw, ...), custom_call_target="tpu_custom_call" | custom-call | tf_op jit(solution)/shard_map/pallas_call | solution.py:575
  101.5 1.1 %convert_bitcast_fusion = f32[16,8,8,256]{3,2,1,0:T(8,128)S(1)} fusion(bf16[16,64,256]{2,1,0:T(8,128)(2,1)} %get-tuple-element.23), kind=kLoop, calls=%fused_computation | loop fusion | flops 262144 | bytes 1572864
  102.6 1.1 %copy.23 = f32[16,8,8,256]{3,2,0,1:T(8,128)} copy(f32[16,8,8,256]{3,2,1,0:T(8,128)S(1)} %convert_bitcast_fusion) | data formatting | bytes 2097152 | tf_op jit(solution)/shard_map/convert_element_type | solution.py:586
  103.7 2.3 %copy.25 = bf16[128,4096]{1,0:T(8,128)(2,1)} copy(bf16[128,4096]{1,0:T(8,128)(2,1)} %get-tuple-element.32) | data formatting | bytes 2097152

commit v2 on v1

--- a/solution.py
+++ b/solution.py
@@ -272,7 +272,7 @@
             sibling(bd, bx).wait_send()
 
 
-def own_slots(slot_row, slot_col, me, tok_dev, row_start, rows):
+def own_slots(slot_row, me, tok_dev, row_start, rows):
     slots = slot_row.shape[1]
     local_row = slot_row - me * tok_dev
     hit = ((local_row >= 0) & (local_row < tok_dev)).astype(f32)
@@ -283,17 +283,17 @@
     rank = jnp.dot(jnp.broadcast_to(hit, (8, slots)).astype(bf16), before, preferred_element_type=f32)[:1]
     wanted = (lax.broadcasted_iota(jnp.int32, (rows, slots), 0) - row_start).astype(f32)
     take = jnp.where(wanted == rank, hit, 0.0)
-    holds = (lax.broadcasted_iota(jnp.int32, (slots, tok_dev), 1) == slot_col - me * tok_dev).astype(f32)
+    holds = (lax.broadcasted_iota(jnp.int32, (tok_dev, slots), 0) == local_row).astype(f32)
     return take.astype(bf16), holds.astype(bf16)
 
 
-def gather_kernel(nd, ne, tok, cot, rw, slot_row, slot_col, rows, probs_out, log_out, load_out,
+def gather_kernel(nd, ne, tok, cot, rw, slot_row, rows, probs_out, log_out, load_out,
                   loads, send_sem, recv_sem, load_send, load_recv):
     place = Place(nd, ne)
     barrier = greet(place)
     tok_dev = tok.shape[0]
-    take, holds = own_slots(slot_row[...], slot_col[...], place.me, tok_dev, 0, PAD)
-    pick = jnp.dot(take, holds, preferred_element_type=f32).astype(bf16)
+    take, holds = own_slots(slot_row[...], place.me, tok_dev, 0, PAD)
+    pick = lax.dot_general(take, holds, NT, preferred_element_type=f32).astype(bf16)
     width = tok.shape[1] // 4
     for part in range(4):
         cols = pl.ds(part * width, width)
@@ -305,7 +305,7 @@
     sends = to_all(place, loads, load_send, load_recv)
 
     def mid():
-        logits = jnp.dot(tok[...], rw[...], preferred_element_type=f32)
+        logits = lax.dot_general(tok[...], rw[...], NT, preferred_element_type=f32)
         top = jnp.max(logits, axis=1, keepdims=True)
         raised = jnp.exp(logits - top)
         total = jnp.sum(raised, axis=1, keepdims=True)
@@ -339,7 +339,7 @@
             ct[span, :] = jnp.concatenate([first[PAD:], second[PAD:]], axis=0).astype(bf16)
         for k in range(width // 512):
             cht[pl.ds(k * 512, 512), :] = ch[:, pl.ds(k * 512, 512)].T
-        logits = jnp.dot(ch[...], rw[...], preferred_element_type=f32)
+        logits = lax.dot_general(ch[...], rw[...], NT, preferred_element_type=f32)
         raised = jnp.exp(logits - jnp.max(logits, axis=1, keepdims=True))
         probs = raised / jnp.sum(raised, axis=1, keepdims=True)
         gate[...] = probs[:, :1]
@@ -461,8 +461,8 @@
                 self.along(bd, p.d).wait_send()
 
 
-def combine_kernel(nd, ne, sums, gate_part, tok, rw, probs_in, log_in, load_in, slot_row, slot_col,
-                   d_tok, d_rout, gates, rpart, s_core, s_one, s_x, s_two, s_z,
+def combine_kernel(nd, ne, sums, gate_part, tok, rw, probs_in, log_in, load_in, slot_row,
+                   d_tok, d_router_t, d_rout, gates, rpart, s_core, s_one, s_x, s_two, s_z,
                    r_core, r_one, r_x, r_two, r_z, gate_send, gate_recv,
                    a0, a1, a2, a3, a4, a5, b0, b1, b2, b3, b4, b5, g_send, g_recv):
     place = Place(nd, ne)
@@ -471,11 +471,10 @@
     tok_dev, experts = probs_in.shape
     slots = gate_part.shape[1]
     gates[me] = gate_part[...]
-    take, holds = own_slots(slot_row[...], slot_col[...], me, tok_dev, 0, PAD)
-    take_all, _ = own_slots(slot_row[...], slot_col[...], me, tok_dev, me * PAD, slots)
-    tn = (((0,), (1,)), ((), ()))
-    place_own = lax.dot_general(holds, take, tn, preferred_element_type=f32).astype(bf16)
-    place_all = lax.dot_general(holds, take_all, tn, preferred_element_type=f32)
+    take, holds = own_slots(slot_row[...], me, tok_dev, 0, PAD)
+    take_all, _ = own_slots(slot_row[...], me, tok_dev, me * PAD, slots)
+    place_own = lax.dot_general(holds, take, NT, preferred_element_type=f32).astype(bf16)
+    place_all = lax.dot_general(holds, take_all, NT, preferred_element_type=f32)
     pl.semaphore_wait(barrier, place.n - 1)
     rows = Scatter(place, sums, s_core, s_one, s_x, s_two, s_z, (a0, a1, a2, a3, a4, a5))
     rout = Scatter(place, rpart, r_core, r_one, r_x, r_two, r_z, (b0, b1, b2, b3, b4, b5))
@@ -502,19 +501,18 @@
     rout.start_across()
     rows.start_along()
     rout.start_along()
+    returned = rows.finish().astype(bf16).astype(f32)
+    for k in range(tok.shape[1] // 256):
+        cols = pl.ds(256 * k, 256)
+        block = returned[PAD * k:PAD * (k + 1)].astype(bf16)
+        d_tok[:, cols] = (
+            jnp.dot(place_own, block, preferred_element_type=f32)
+            + jnp.dot(lg, rw[:, cols], preferred_element_type=f32)
+        ).astype(bf16)
     d_rout[me] = rout.finish().astype(bf16)
-
-    def mid():
-        returned = rows.finish().astype(bf16).astype(f32)
-        for k in range(tok.shape[1] // 256):
-            cols = pl.ds(256 * k, 256)
-            block = returned[PAD * k:PAD * (k + 1)].astype(bf16)
-            d_tok[:, cols] = (
-                jnp.dot(place_own, block, preferred_element_type=f32)
-                + lax.dot_general(lg, rw[cols, :], NT, preferred_element_type=f32)
-            ).astype(bf16)
-
-    gather_blocks(place, d_rout, g_send, g_recv, mid)
+    gather_blocks(place, d_rout, g_send, g_recv)
+    for owner in range(place.n):
+        d_router_t[:, pl.ds(256 * owner, 256)] = d_rout[owner].astype(f32)
     rows.drain()
     rout.drain()
     for send in gate_sends:
@@ -525,10 +523,11 @@
     tok_dev, width = tokens.shape
     experts = router_weight.shape[1]
     ff = w_gate.shape[1]
+    router_t = router_weight.T
     owners = nd * ne
     slots = owners * PAD
     nx = ne // 2
-    slot_row, slot_col = slot_token[None, :], slot_token[:, None]
+    slot_row = slot_token[None, :]
     vmem = pl.BlockSpec(memory_space=pltpu.VMEM)
     dma = pltpu.SemaphoreType.DMA
     sds = jax.ShapeDtypeStruct
@@ -537,13 +536,13 @@
         functools.partial(gather_kernel, nd, ne),
         out_shape=(sds((owners, 2 * PAD, width), bf16), sds((tok_dev, experts), f32),
                    sds((tok_dev, 1), f32), sds((8, experts), f32)),
-        in_specs=[vmem] * 5,
+        in_specs=[vmem] * 4,
         out_specs=(vmem,) * 4,
         scratch_shapes=[pltpu.VMEM((owners, 8, experts), f32), dma((4, owners)), dma((owners,)),
                         dma((owners - 1,)), dma((owners,))],
         compiler_params=pltpu.CompilerParams(
             collective_id=0, has_side_effects=True, vmem_limit_bytes=limit),
-    )(tokens, cotangent, router_weight, slot_row, slot_col)
+    )(tokens, cotangent, router_t, slot_row)
 
     tile = 256
     steps = ff // tile
@@ -555,14 +554,14 @@
         grid=(steps,),
         out_shape=(sds(w_gate.shape, bf16), sds(w_up.shape, bf16), sds(w_down.shape, bf16),
                    sds((2, nx, nd, PAD * width // 256, 256), bf16), sds((8, slots), f32)),
-        in_specs=[whole(owners, 2 * PAD, width), whole(width, experts), columns, columns, lines],
+        in_specs=[whole(owners, 2 * PAD, width), whole(experts, width), columns, columns, lines],
         out_specs=(columns, columns, lines, whole(2, nx, nd, PAD * width // 256, 256), whole(8, slots)),
         scratch_shapes=[pltpu.VMEM((slots, width), bf16), pltpu.VMEM((width, slots), bf16),
                         pltpu.VMEM((slots, width), bf16), pltpu.VMEM((slots, width), bf16),
                         pltpu.VMEM((slots, 1), f32), pltpu.VMEM((slots, width), f32),
                         pltpu.VMEM((slots, 1), f32)],
         compiler_params=pltpu.CompilerParams(vmem_limit_bytes=limit),
-    )(rows, router_weight, w_gate, w_up, w_down)
+    )(rows, router_t, w_gate, w_up, w_down)
 
     sblock, rblock = (PAD * width // 256, 256), (experts, 256)
 
@@ -572,19 +571,19 @@
                 pltpu.VMEM((nd,) + block, kind)]
 
     stage_sems = [dma((nx,)), dma((nx,)), dma((nd,)), dma((nd,)), dma((nd,)), dma((nd,))]
-    d_tokens, d_rout = pl.pallas_call(
+    d_tokens, d_router_t = pl.pallas_call(
         functools.partial(combine_kernel, nd, ne),
-        out_shape=(sds((tok_dev, width), bf16), sds((owners, experts, 256), bf16)),
-        in_specs=[vmem] * 9,
+        out_shape=(sds((tok_dev, width), bf16), sds((experts, width), f32)),
+        in_specs=[vmem] * 8,
         out_specs=(vmem,) * 2,
-        scratch_shapes=[pltpu.VMEM((owners, 8, slots), f32), pltpu.VMEM((2, nx, nd) + rblock, f32)]
+        scratch_shapes=[pltpu.VMEM((owners, experts, 256), bf16),
+                        pltpu.VMEM((owners, 8, slots), f32), pltpu.VMEM((2, nx, nd) + rblock, f32)]
         + stages(sblock, bf16) + stages(rblock, f32) + [dma((owners - 1,)), dma((owners,))]
         + stage_sems + stage_sems + [dma((4, owners)), dma((owners,))],
         compiler_params=pltpu.CompilerParams(
             collective_id=1, has_side_effects=True, vmem_limit_bytes=limit),
-    )(sums, gate_part, tokens, router_weight, probs, log_total, load, slot_row, slot_col)
-    d_router = jnp.transpose(d_rout, (0, 2, 1)).reshape(width, experts).astype(f32)
-    return d_tokens, d_router, d_w_gate, d_w_up, d_w_down
+    )(sums, gate_part, tokens, router_t, probs, log_total, load, slot_row)
+    return d_tokens, d_router_t.T, d_w_gate, d_w_up, d_w_down
 
 
 def solution(mesh):

time: 106 us -> 102 us (0.962)
  local copies, waits for them, and re-layouts: 7.07 us -> 4.56 us
  other arithmetic: 1.15 us -> 0 us
    broadcast_in_dim x1 -> x0, local copies, waits for them, and re-layouts: 1.36 us -> none  [fast_local(): slot_row, slot_col = (slot_token[None, :], slot_token[:, None])]
    unnamed x1 -> x0, other arithmetic: 1.15 us -> none
    convert_element_type x1 -> x0, local copies, waits for them, and re-layouts: 1.07 us -> none  [fast_local(): jnp.transpose(d_rout, (0, 2, 1)).reshape(width, experts).astype(f32)]
where the time goes in v2:
time: 102 us
  Pallas kernels  96.8 us (95%)
  local copies, waits for them, and re-layouts  4.56 us (4%)
    pallas_call x1, Pallas kernels, fast_local(): pl.pallas_call(functools.partial(combine_kernel, nd, ne), out_shape=(sds(...  41.5 us
    pallas_call x1, Pallas kernels, fast_local(): pl.pallas_call(functools.partial(expert_kernel, steps, nd, ne), grid=(ste...  28 us
    pallas_call x1, Pallas kernels, fast_local(): pl.pallas_call(functools.partial(gather_kernel, nd, ne), out_shape=(sds((...  27.2 us
    unnamed x2, local copies, waits for them, and re-layouts  4.56 us

profile of v2, /device:TPU:0, one launch (start us, length us, event | category | flops | bytes accessed | tf_op | source)
XLA Modules:
  0.0 102.0 jit_solution(14589255790857616891)
XLA Ops:
  0.6 27.2 %shard_map.110 = (bf16[16,16,4096]{2,1,0:T(8,128)(2,1)}, f32[128,64]{1,0:T(8,128)}, f32[128,1]{1,0:T(8,128)}, f32[8,64]{1,0:T(8,128)}) custom-call(bf16[128,4096]{1,0:T(8,128)(2,1)} %tok.3, bf16[128,4096]{1,0:T(8,128)(2,1)} %cot.1, bf16[64,4096]{1,0:T(8,128)(2,1)} %bitcast.3, s32[1,64]{1,0:T(1,128)} %bitcast.7), custom_call_target="tpu_custom_call" | custom-call | tf_op jit(solution)/shard_map/pallas_call | solution.py:535
  27.9 28.0 %shard_map.111 = (bf16[4096,1024]{1,0:T(8,128)(2,1)}, bf16[4096,1024]{1,0:T(8,128)(2,1)}, bf16[1024,4096]{1,0:T(8,128)(2,1)}, bf16[2,2,4,128,256]{4,3,2,1,0:T(8,128)(2,1)}, f32[8,128]{1,0:T(8,128)}) custom-call(bf16[16,16,4096]{2,1,0:T(8,128)(2,1)} %get-tuple-element.16.rows, bf16[64,4096]{1,0:T(8,128)(2,1)} %bitcast.4, bf16[4096,1024]{1,0:T(8,128)(2,1)} %wg.1, ...), custom_call_target="tpu_custom_call" | custom-call | tf_op jit(solution)/shard_map/pallas_call | solution.py:552
  55.9 41.5 %shard_map.112 = (bf16[128,4096]{1,0:T(8,128)(2,1)}, f32[64,4096]{1,0:T(8,128)}) custom-call(bf16[2,2,4,128,256]{4,3,2,1,0:T(8,128)(2,1)} %get-tuple-element.17.sums, f32[8,128]{1,0:T(8,128)} %get-tuple-element.18.gate_part, bf16[128,4096]{1,0:T(8,128)(2,1)} %tok.3, bf16[64,4096]{1,0:T(8,128)(2,1)} %bitcast.5, f32[128,64]{1,0:T(8,128)} %get-tuple-element.19.probs_in, ...), custom_call_target="tpu_custom_call" | custom-call | tf_op jit(solution)/shard_map/pallas_call | solution.py:574
  97.4 2.3 %copy.14 = bf16[128,4096]{1,0:T(8,128)(2,1)} copy(bf16[128,4096]{1,0:T(8,128)(2,1)} %get-tuple-element.32) | data formatting | bytes 2097152
  99.7 2.3 %copy.15 = f32[4096,64]{0,1:T(8,128)} copy(f32[4096,64]{0,1:T(8,128)} %bitcast.6) | data formatting | bytes 2097152
